TPU v7x, 32 devices: a whole 2x2x4 slice. The times are simulated.
32 devices in a mesh: groups: 2 (over y), dp: 4 (over x, core), tensor: 4 (over z).
Axes of the slice: x: 2, y: 2, z: 4, core: 2. Of those that a mesh axis runs over, the one named last changes fastest.
Arguments:
- output_gradient: bfloat16 [4096, 8192], P(('groups', 'dp', 'tensor')), parts along dimension 0, may hold values from -6 to 6
- attention_input: bfloat16 [4096, 8192], P(('groups', 'dp'), 'tensor'), parts along dimension 0, may hold values from -6 to 6
- output_weight: bfloat16 [8192, 8192], P('tensor'), may hold values from -0.0625 to 0.0625
- adapter_down_weight: bfloat16 [16, 8192, 16], P('dp', 'tensor'), may hold values from -0.0625 to 0.0625
- adapter_up_weight: bfloat16 [16, 16, 8192], P('dp', None, 'tensor'), may hold values from -0.125 to 0.125
- tenant_of_block: int32 [32], P(('groups', 'dp')), parts along dimension 0, may hold values from 0 to 15
- slot_of_tenant: int32 [16], replicated, may hold values from 0 to 15, each once
Outputs:
- grad_in: bfloat16 [4096, 8192], P(('groups', 'dp'), 'tensor'), parts along dimension 0
- down_gradient: float32 [32, 8192, 16], P(('groups', 'dp'), 'tensor'), parts along dimension 0
- up_gradient: float32 [32, 16, 8192], P(('groups', 'dp'), None, 'tensor'), parts along dimension 0
There are 2 independent parts, one for each index of `groups`. A program takes and returns all parts, laid end to end along the dimension named above; an argument that names none is the same for every part. Nothing has to cross between parts.
All inputs are finite; a program needn't handle non-finite values.
Results may differ from a plain program's by a relative error of at most 0.0034.
Values may be sent and summed in bfloat16 or wider, within the bound.
A program may use at most 128 MiB of HBM per device.

v0:
```python
import jax
import jax.numpy as jnp
from jax import lax
from jax.sharding import PartitionSpec as P

adapter_scale = 2.0


def body(
    output_gradient,
    attention_input,
    output_weight,
    adapter_down_weight,
    adapter_up_weight,
    tenant_of_block,
    slot_of_tenant,
):
    block_count = tenant_of_block.shape[0]
    shard_rows, local_width = attention_input.shape
    rows_per_block = shard_rows // block_count
    held_slot_count = adapter_down_weight.shape[0]
    width_of_rank = adapter_down_weight.shape[2]
    down_all, up_all = (
        lax.all_gather(adapter_down_weight.reshape(held_slot_count, -1), "dp", axis=0, tiled=True),
        lax.all_gather(adapter_up_weight.reshape(held_slot_count, -1), "dp", axis=0, tiled=True),
    )
    slot_of_block = jnp.take(slot_of_tenant, tenant_of_block)
    selected_down = jnp.take(down_all, slot_of_block, axis=0).reshape(
        block_count, local_width, width_of_rank
    )
    selected_up = jnp.take(up_all, slot_of_block, axis=0).reshape(
        block_count, width_of_rank, local_width
    )
    in_blocks = attention_input.reshape(block_count, rows_per_block, local_width)
    down_part = jnp.einsum(
        "bnd,bdr->bnr", in_blocks, selected_down, preferred_element_type=jnp.float32
    )
    down_flattened = lax.psum(down_part.reshape(block_count, -1), "tensor")
    col_first = lax.axis_index("tensor") * local_width
    rows_piece = lax.all_gather(output_gradient, "tensor", axis=0, tiled=True)
    base_rows = jnp.einsum(
        "kd,hd->kh", rows_piece, output_weight, preferred_element_type=jnp.float32
    )
    own_cols = lax.dynamic_slice_in_dim(rows_piece, col_first, local_width, 1)
    joined = jnp.concatenate([base_rows, own_cols.astype(jnp.float32)], axis=1)
    base_part = joined[:, :local_width]
    dy_blocks = (
        joined[:, local_width:]
        .astype(jnp.bfloat16)
        .reshape(block_count, rows_per_block, local_width)
    )
    up_part = jnp.einsum("bnc,brc->bnr", dy_blocks, selected_up, preferred_element_type=jnp.float32)
    up_flattened = lax.psum(up_part.reshape(block_count, -1), "tensor")
    scaled_up_result = (
        adapter_scale * up_flattened.reshape(block_count, rows_per_block, width_of_rank)
    ).astype(jnp.bfloat16)
    scaled_down_result = (
        adapter_scale * down_flattened.reshape(block_count, rows_per_block, width_of_rank)
    ).astype(jnp.bfloat16)
    extra = jnp.einsum(
        "bnr,bdr->bnd", scaled_up_result, selected_down, preferred_element_type=jnp.float32
    )
    grad_in = (base_part + extra.reshape(shard_rows, local_width)).astype(jnp.bfloat16)
    down_by_block = jnp.einsum(
        "bnd,bnr->bdr", in_blocks, scaled_up_result, preferred_element_type=jnp.float32
    ).reshape(block_count, -1)
    up_by_block = jnp.einsum(
        "bnr,bnc->brc", scaled_down_result, dy_blocks, preferred_element_type=jnp.float32
    ).reshape(block_count, -1)
    every_down, every_up, every_slot = (
        lax.all_gather(down_by_block, "dp", axis=0, tiled=True),
        lax.all_gather(up_by_block, "dp", axis=0, tiled=True),
        lax.all_gather(slot_of_block.astype(jnp.float32), "dp", axis=0, tiled=True),
    )
    my_slots = (
        lax.axis_index("dp") * held_slot_count + jnp.arange(held_slot_count, dtype=jnp.int32)
    ).astype(jnp.float32)
    selector = (my_slots[:, None] == every_slot[None, :]).astype(jnp.float32)
    down_gradient = jnp.dot(selector, every_down, precision=lax.Precision.HIGHEST)
    up_gradient = jnp.dot(selector, every_up, precision=lax.Precision.HIGHEST)
    down_gradient = down_gradient.reshape(held_slot_count, local_width, width_of_rank)
    up_gradient = up_gradient.reshape(held_slot_count, width_of_rank, local_width)
    return (grad_in, down_gradient, up_gradient)


def solution(mesh):
    in_specs = (
        P(("groups", "dp", "tensor"), None),
        P(("groups", "dp"), "tensor"),
        P("tensor", None),
        P("dp", "tensor", None),
        P("dp", None, "tensor"),
        P(("groups", "dp")),
        P(),
    )
    out_specs = (
        P(("groups", "dp"), "tensor"),
        P(("groups", "dp"), "tensor", None),
        P(("groups", "dp"), None, "tensor"),
    )
    return jax.shard_map(body, mesh=mesh, in_specs=in_specs, out_specs=out_specs, check_vma=False)
```

profile of v0, /device:TPU:0, one launch (start us, length us, event | category | flops | bytes accessed | tf_op | source)
XLA Modules:
  0.0 309.8 jit_solution(2723164660698918129)
XLA Ops:
  7.2 0.0 all-gather.14.cloned.1.call-start
  7.2 2.7 copy.24
  10.0 4.7 %reshape.114 = bf16[1,4,32768]{2,1,0:T(4,128)(2,1)} reshape(bf16[4,2048,16]{2,1,0:T(8,128)(2,1)} %copy.24) | data formatting | bytes 524288
  14.7 0.0 all-gather.12.cloned.1.call-start
  14.8 0.9 reshape.112
  15.7 0.0 all-gather.10.cloned.1.call-start
  15.7 0.7 all-gather.10.cloned.1.call-update
  16.4 0.0 all-reduce.4.cloned.1.call-start
  16.5 0.6 gather_fusion
  17.2 17.1 %all-gather.14.cloned.1.call-done = bf16[4,4,32768]{2,1,0:T(4,128)(2,1)} async-done(((bf16[1,4,32768]{2,1,0:T(4,128)(2,1)}), bf16[4,4,32768]{2,1,0:T(4,128)(2,1)}) %all-gather.14.cloned.1.call-update) | async-done | bytes 1048592 | tf_op jit(solution)/shard_map/all_gather | solution.py:24
  34.3 1.4 reshape.115
  35.7 0.8 gather_fusion.2
  36.5 16.7 %all-gather.12.cloned.1.call-done = bf16[4,4,32768]{2,1,0:T(4,128)(2,1)} async-done(((bf16[1,4,32768]{2,1,0:T(4,128)(2,1)}), bf16[4,4,32768]{2,1,0:T(4,128)(2,1)}) %all-gather.12.cloned.1.call-update) | async-done | bytes 1048592 | tf_op jit(solution)/shard_map/all_gather | solution.py:25
  53.2 1.4 reshape.113
  54.6 1.5 gather_fusion.1
  56.0 1.2 broadcast_select_fusion
  57.3 2.8 reshape.74
  60.1 2.6 convolution_bitcast_fusion.1
  62.8 0.1 copy.30
  62.9 0.8 reshape.79
  63.7 140.7 %all-gather.10.cloned.1.call-done = bf16[512,8192]{1,0:T(8,128)(2,1)} async-done(((bf16[128,8192]{1,0:T(8,128)(2,1)}), bf16[512,8192]{1,0:T(8,128)(2,1)}) %all-gather.10.cloned.1.call-update) | async-done | bytes 8388624 | tf_op jit(solution)/shard_map/all_gather | solution.py:40
  204.4 1.7 constant_dynamic-slice_fusion
  206.2 1.4 copy-done.4
  207.6 0.7 fusion.1
  208.3 0.8 reshape.72
  209.1 0.0 all-gather.18.cloned.1.call-start
  209.1 32.4 %all-reduce.4.cloned.1.call-done = (f32[4,2048]{1,0:T(4,128)}, f32[4,2048]{1,0:T(4,128)}) async-done(((f32[4,2048]{1,0:T(4,128)}, f32[4,2048]{1,0:T(4,128)}), (f32[4,2048]{1,0:T(4,128)}, f32[4,2048]{1,0:T(4,128)})) %all-reduce.4.cloned.1.call-update) | async-done | bytes 65552 | tf_op jit(solution)/shard_map/psum | solution.py:53
  241.5 0.8 multiply_convert_fusion
  242.3 0.1 convert_element_type.34
  242.5 2.0 fusion.13
  244.5 1.2 reshape.118
  245.7 0.0 all-gather.16.cloned.1.call-start
  245.8 0.6 dynamic-slice
  247.0 0.1 convert_dynamic-update-slice_fusion
  247.1 5.8 %all-reduce = f32[16]{0:T(128)S(1)} all-reduce(f32[16]{0:T(128)S(1)} %convert_dynamic-update-slice_fusion), channel_id=1, replica_groups=mesh['groups'=2,'dp'=4,'tensor'=4] {'dp'}, use_global_device_ids=true, to_apply=%add | all-reduce | flops 16 | bytes 128
  253.0 0.1 convert_element_type.29
  253.1 0.4 convolution_bitcast_fusion
  253.5 2.7 copy.28
  256.2 5.3 %reshape.116 = f32[1,4,32768]{2,1,0:T(4,128)} reshape(f32[4,2048,16]{2,1,0:T(8,128)} %copy.28) | data formatting | bytes 1048576
  261.5 2.7 fusion.12
  264.2 25.1 %fusion = bf16[512,2048]{1,0:T(8,128)(2,1)} fusion(f32[4,128,2048]{2,1,0:T(8,128)} %fusion.12, bf16[512,8192]{1,0:T(8,128)(2,1)} %all-gather.10.cloned.1.call-done, bf16[2048,8192]{1,0:T(8,128)(2,1)} %param.11), kind=kOutput, calls=%fused_computation.4 | convolution fusion | flops 17181966336 | bytes 48234496 | tf_op jit(solution)/shard_map/kd,hd->kh/dot_general | solution.py:41
  289.3 2.0 reshape.119
  291.3 0.8 fusion.4
  292.1 1.1 copy.46
  293.2 2.0 reshape.117
  295.2 0.8 fusion.6
  296.0 3.4 %reshape.78 = f32[4,2048,16]{2,1,0:T(8,128)} reshape(f32[4,32768]{1,0:T(4,128)S(1)} %fusion.6) | data formatting | bytes 1048576 | tf_op jit(solution)/shard_map/reshape | solution.py:81
  299.4 3.5 %copy.32 = f32[4,2048,16]{1,2,0:T(8,128)} copy(f32[4,2048,16]{2,1,0:T(8,128)} %reshape.78) | data formatting | bytes 1048576
  (28 shorter events, 0.2 us)
Async XLA Ops:
  7.2 53.0 %copy-start = (bf16[512,2048]{1,0:T(8,128)(2,1)S(1)}, bf16[512,2048]{1,0:T(8,128)(2,1)}, u32[]{:S(2)}) copy-start(bf16[512,2048]{1,0:T(8,128)(2,1)} %param.10) | copy-start | bytes 6291460
  7.2 7.6 %copy-start.5 = (bf16[4,16,2048]{2,1,0:T(8,128)(2,1)S(1)}, bf16[4,16,2048]{2,1,0:T(8,128)(2,1)}, u32[]{:S(2)}) copy-start(bf16[4,16,2048]{2,1,0:T(8,128)(2,1)} %param.13) | copy-start | bytes 786436
  7.2 27.1 %all-gather.14.cloned.1.call-start = ((), (), s32[]{:S(2)}) async-start(), calls=%async_computation.2 | async-start | bytes 1310720 | tf_op jit(solution)/shard_map/all_gather | solution.py:24
  14.7 1.8 copy-start.6
  14.7 1.8 copy-start.2
  14.7 38.5 %all-gather.12.cloned.1.call-start = ((), (), s32[]{:S(2)}) async-start(), calls=%async_computation.1 | async-start | bytes 1310720 | tf_op jit(solution)/shard_map/all_gather | solution.py:25
  15.7 188.7 %all-gather.10.cloned.1.call-start = ((), (), s32[]{:S(2)}) async-start(), calls=%async_computation | async-start | bytes 10485760 | tf_op jit(solution)/shard_map/all_gather | solution.py:40
  16.4 225.1 %all-reduce.4.cloned.1.call-start = ((), (), s32[]{:S(2)}) async-start(), calls=%async_computation.5 | async-start | bytes 131072 | tf_op jit(solution)/shard_map/psum | solution.py:53
  206.2 1.4 copy-start.4
  209.1 80.2 %all-gather.18.cloned.1.call-start = ((), (), s32[]{:S(2)}) async-start(), calls=%async_computation.4 | async-start | bytes 2621440 | tf_op jit(solution)/shard_map/all_gather | solution.py:72
  242.5 3.3 %copy-start.7 = (u32[32]{0:T(128)S(1)}, u32[32]{0:T(128)}, u32[]{:S(2)}) copy-start(u32[32]{0:T(128)} %constant.45) | copy-start | bytes 388
  245.7 47.5 %all-gather.16.cloned.1.call-start = ((), (), s32[]{:S(2)}) async-start(), calls=%async_computation.3 | async-start | bytes 2621440 | tf_op jit(solution)/shard_map/all_gather | solution.py:71
  256.2 5.3 %copy-start.3 = (bf16[4,2048,16]{2,1,0:T(8,128)(2,1)S(1)}, bf16[4,2048,16]{2,1,0:T(8,128)(2,1)}, u32[]{:S(2)}) copy-start(bf16[4,2048,16]{2,1,0:T(8,128)(2,1)} %reshape.74) | copy-start | bytes 786436
  296.0 6.9 %copy-start.1 = (bf16[512,2048]{1,0:T(8,128)(2,1)S(1)}, bf16[512,2048]{1,0:T(8,128)(2,1)}, u32[]{:S(2)}) copy-start(bf16[512,2048]{1,0:T(8,128)(2,1)} %param.10) | copy-start | bytes 6291460
Sparse Core Ops, SparseCore 0:
  14.8 19.4 all-gather.13
  36.4 16.7 all-gather.11
  54.8 149.6 all-gather.9
  209.2 32.2 all-reduce.3
  245.8 22.2 all-gather.17
  270.2 22.5 all-gather.15
where the time goes:
time: 310 us
  waiting for transfers between devices  208 us (67%)
  local copies, waits for them, and re-layouts  43.6 us (14%)
  matrix products  35.2 us (11%)
  between operations  15 us (5%)
  blocking collectives  5.81 us (2%)
    all_gather x1, waiting for transfers between devices, body(): rows_piece = lax.all_gather(output_gradient, 'tensor', axis=0, tiled=True)  141 us
    psum x1, waiting for transfers between devices, body(): up_flattened = lax.psum(up_part.reshape(block_count, -1), 'tensor')  32.4 us
    unnamed x29, local copies, waits for them, and re-layouts  28.1 us
    dot_general x1, matrix products, body(): jnp.einsum('kd,hd->kh', rows_piece, output_weight, preferred_element_type...  25.1 us
    all_gather x1, waiting for transfers between devices, body(): lax.all_gather(adapter_down_weight.reshape(held_slot_count, -1), 'dp', ax...  17.1 us
    all_gather x1, waiting for transfers between devices, body(): lax.all_gather(adapter_up_weight.reshape(held_slot_count, -1), 'dp', axis...  16.7 us
  transfers between devices with their start and end apart: 6, of which 4 were waited for; matrix products, arithmetic and copies ran while one was open for 18% of the time, Pallas kernels for 0%

commit v1 on v0

v1 whole, which is shorter than its diff:
```python
import functools

import jax
import jax.numpy as jnp
from jax import lax
from jax.experimental import pallas as pl
from jax.experimental.pallas import tpu as pltpu
from jax.sharding import PartitionSpec as P

adapter_scale = 2.0
MESH = pl.DeviceIdType.MESH
NT = (((1,), (1,)), ((), ()))
NN = (((1,), (0,)), ((), ()))
TN = (((0,), (0,)), ((), ()))


def dot(a, b, dims):
    return lax.dot_general(a, b, dims, preferred_element_type=jnp.float32)


def kernel(
    n,
    dp,
    chunks,
    slots_ref,
    pick_ref,
    adapters_ref,
    dy_ref,
    x_ref,
    w_ref,
    out_ref,
    grads_ref,
    w_v,
    rows_v,
    acc,
    x_v,
    all_adapters,
    selected,
    up_own,
    down_send,
    down_recv,
    ups,
    outer_send,
    outer_recv,
    by_block,
    share_send,
    share_recv,
    total,
    out_v,
    w_sem,
    x_sem,
    dy_sem,
    hop_send,
    hop_recv,
    a_send,
    a_recv,
    z_send,
    z_recv,
    s_send,
    s_recv,
    out_sem,
    grads_sem,
):
    f32, bf16 = jnp.float32, jnp.bfloat16
    me, me_dp = lax.axis_index("tensor"), lax.axis_index("dp")
    own_rows = dy_ref.shape[0]
    shard_rows, local = x_ref.shape
    chunk = dy_ref.shape[1] // chunks
    held, rank = adapters_ref.shape[0], adapters_ref.shape[1] // 2
    blocks = slots_ref.shape[0]
    per_block = n // blocks

    dy_in = [
        pltpu.make_async_copy(dy_ref.at[:, pl.ds(c * chunk, chunk)], rows_v.at[me, c], dy_sem.at[c])
        for c in range(chunks)
    ]
    for copy in dy_in:
        copy.start()
    x_in = pltpu.make_async_copy(x_ref, x_v, x_sem)
    x_in.start()
    w_in = [
        pltpu.make_async_copy(w_ref.at[:, pl.ds(c * chunk, chunk)], w_v.at[c], w_sem.at[c])
        for c in range(chunks)
    ]
    for copy in w_in:
        copy.start()

    barrier = pltpu.get_barrier_semaphore()
    for k in range(1, n):
        pl.semaphore_signal(
            barrier, inc=1, device_id={"tensor": lax.rem(me + k, n)}, device_id_type=MESH
        )
    for k in range(1, dp):
        pl.semaphore_signal(
            barrier, inc=1, device_id={"dp": lax.rem(me_dp + k, dp)}, device_id_type=MESH
        )
    pl.semaphore_wait(barrier, n - 1 + dp - 1)

    def hop(way, step, c):
        shard = jnp.clip(me - step if way == 0 else me + step, 0, n - 1)
        to = jnp.minimum(me + 1, n - 1) if way == 0 else jnp.maximum(me - 1, 0)
        return pltpu.make_async_remote_copy(
            src_ref=rows_v.at[shard, c],
            dst_ref=rows_v.at[shard, c],
            send_sem=hop_send.at[way, step, c],
            recv_sem=hop_recv.at[way, step, c],
            device_id={"tensor": to},
            device_id_type=MESH,
        )

    def sends(way, step):
        return (me >= step) & (me < n - 1) if way == 0 else (me + step <= n - 1) & (me > 0)

    def receives(way, step):
        return me >= step + 1 if way == 0 else me + step + 1 <= n - 1

    def incoming(way, step):
        return jnp.clip(me - 1 - step if way == 0 else me + 1 + step, 0, n - 1)

    def arrived(way, step, c):
        shard = incoming(way, step)
        return pltpu.make_async_remote_copy(
            src_ref=rows_v.at[shard, c],
            dst_ref=rows_v.at[shard, c],
            send_sem=hop_send.at[way, step, c],
            recv_sem=hop_recv.at[way, step, c],
            device_id={"tensor": jnp.minimum(me + 1, n - 1) if way == 0 else jnp.maximum(me - 1, 0)},
            device_id_type=MESH,
        )

    for c in range(chunks):
        dy_in[c].wait()
        for way in range(2):

            @pl.when(sends(way, 0))
            def _(way=way, c=c):
                hop(way, 0, c).start()

    def adapters_copy(k):
        peer = lax.rem(me_dp + k, dp)
        return pltpu.make_async_remote_copy(
            src_ref=adapters_ref,
            dst_ref=all_adapters.at[pl.ds(me_dp * held, held)],
            send_sem=a_send.at[k - 1],
            recv_sem=a_recv.at[k - 1],
            device_id={"dp": peer},
            device_id_type=MESH,
        )

    def adapters_arrival(k):
        source = lax.rem(me_dp + dp - k, dp)
        return pltpu.make_async_remote_copy(
            src_ref=adapters_ref,
            dst_ref=all_adapters.at[pl.ds(source * held, held)],
            send_sem=a_send.at[k - 1],
            recv_sem=a_recv.at[k - 1],
            device_id={"dp": source},
            device_id_type=MESH,
        )

    for k in range(1, dp):
        adapters_copy(k).start()
    all_adapters[pl.ds(me_dp * held, held)] = adapters_ref[...]

    def z_copy(kind, k, arrival=False):
        peer = lax.rem(me + (n - k if arrival else k), n)
        slot = peer if arrival else me
        source, target = {
            0: (lambda p: selected.at[p // per_block, pl.ds(rank, rank)], up_own),
            1: (lambda p: down_send.at[p], down_recv),
            2: (lambda p: ups.at[me], ups),
            3: (lambda p: outer_send.at[p], outer_recv),
        }[kind]
        return pltpu.make_async_remote_copy(
            src_ref=source(peer),
            dst_ref=target.at[slot],
            send_sem=z_send.at[kind, k - 1],
            recv_sem=z_recv.at[kind, k - 1],
            device_id={"tensor": peer},
            device_id_type=MESH,
        )

    def z_start(kind):
        for k in range(1, n):
            z_copy(kind, k).start()

    def z_wait(kind):
        for k in range(1, n):
            z_copy(kind, k, True).wait_recv()

    def share_copy(k, arrival=False):
        peer = lax.rem(me_dp + (dp - k if arrival else k), dp)
        return pltpu.make_async_remote_copy(
            src_ref=share_send.at[peer],
            dst_ref=share_recv.at[peer if arrival else me_dp],
            send_sem=s_send.at[k - 1],
            recv_sem=s_recv.at[k - 1],
            device_id={"dp": peer},
            device_id_type=MESH,
        )

    def own_features(t):
        return t * local // chunk, pl.ds(t * local % chunk, local)

    def select():
        for k in range(1, dp):
            adapters_arrival(k).wait_recv()
        for b in range(blocks):
            selected[b] = all_adapters[slots_ref[b]]
        z_start(0)
        x_in.wait()
        for t in range(n):
            down_send[t] = dot(
                selected[t // per_block, 0:rank], x_v[t * own_rows : (t + 1) * own_rows, :], NT
            )
        z_start(1)

    def activations():
        z_wait(0)
        z_wait(1)
        up_own[me] = selected[me // per_block, pl.ds(rank, rank)]
        down_recv[me] = down_send[me]
        up = jnp.zeros((rank, own_rows), f32)
        down = jnp.zeros((rank, own_rows), f32)
        for t in range(n):
            c, columns = own_features(t)
            up = up + dot(up_own[t], rows_v[me, c, :, columns], NT)
            down = down + down_recv[t]
        ups[me] = (adapter_scale * up).astype(bf16)
        z_start(2)
        down = (adapter_scale * down).astype(bf16)
        for t in range(n):
            c, columns = own_features(t)
            outer_send[t] = dot(down, rows_v[me, c, :, columns], NN).astype(bf16)
        z_start(3)

    def gradients():
        z_wait(2)
        z_wait(3)
        outer_recv[me] = outer_send[me]
        for b in range(blocks):
            down_sum = jnp.zeros((rank, local), f32)
            up_sum = jnp.zeros((rank, local), f32)
            for t in range(b * per_block, (b + 1) * per_block):
                down_sum = down_sum + dot(ups[t], x_v[t * own_rows : (t + 1) * own_rows, :], NN)
                up_sum = up_sum + outer_recv[t].astype(f32)
            by_block[b, 0:rank] = down_sum
            by_block[b, rank : 2 * rank] = up_sum

        def share(slot):
            value = pick_ref[slot, 0] * by_block[0]
            for b in range(1, blocks):
                value = value + pick_ref[slot, b] * by_block[b]
            return value

        for k in range(1, dp):
            peer = lax.rem(me_dp + k, dp)
            for s in range(held):
                share_send[peer, s] = share(peer * held + s).astype(bf16)
            share_copy(k).start()
        for s in range(held):
            total[s] = share(me_dp * held + s)
        for t in range(n):
            acc[t] += dot(ups[t], selected[t // per_block, 0:rank], TN)

    def owners():
        for k in range(1, dp):
            share_copy(k, True).wait_recv()
            source = lax.rem(me_dp + dp - k, dp)
            for s in range(held):
                total[s] += share_recv[source, s].astype(f32)
        pltpu.make_async_copy(total, grads_ref, grads_sem).start()

    tile = min(512, local)

    def multiply(shard, c):
        @pl.loop(0, local // tile)
        def _(i):
            at = pl.ds(pl.multiple_of(i * tile, tile), tile)
            acc[shard, :, at] += dot(rows_v[shard, c], w_v[c, at, :], NT)

    def out_copy(shard):
        return pltpu.make_async_copy(
            out_v.at[shard], out_ref.at[pl.ds(shard * own_rows, own_rows)], out_sem.at[shard]
        )

    def finish(shard):
        out_v[shard] = acc[shard].astype(bf16)
        out_copy(shard).start()

    acc[...] = jnp.zeros_like(acc)
    for c in range(chunks):
        w_in[c].wait()
        multiply(me, c)

    phases = {1: select, 3: activations, 5: gradients, 9: owners}
    ready, waiting, event = False, [(None, None)], 0
    last_phase = 9

    def flush(items):
        for way, step in items:
            if way is None:
                finish(me)
            else:

                @pl.when(receives(way, step))
                def _(way=way, step=step):
                    finish(incoming(way, step))

    for step in range(n - 1):
        for c in range(chunks):
            for way in range(2):

                @pl.when(receives(way, step))
                def _(way=way, step=step, c=c):
                    arrived(way, step, c).wait_recv()
                    if step + 1 < n - 1:

                        @pl.when(sends(way, step + 1))
                        def _():
                            hop(way, step + 1, c).start()

            for way in range(2):

                @pl.when(receives(way, step))
                def _(way=way, step=step, c=c):
                    multiply(incoming(way, step), c)

            if event in phases:
                phases[event]()
                if event == 5:
                    ready = True
            event += 1
        waiting += [(0, step), (1, step)]
        if ready:
            flush(waiting)
            waiting = []
    for step in range(n - 1):
        for way in range(2):
            for c in range(chunks):

                @pl.when(sends(way, step))
                def _(way=way, step=step, c=c):
                    hop(way, step, c).wait_send()

    for k in range(1, dp):
        adapters_copy(k).wait_send()
        share_copy(k).wait_send()
    for kind in range(4):
        for k in range(1, n):
            z_copy(kind, k).wait_send()
    pltpu.make_async_copy(total, grads_ref, grads_sem).wait()
    for t in range(n):
        out_copy(t).wait()


def body(
    n,
    dp,
    output_gradient,
    attention_input,
    output_weight,
    adapter_down_weight,
    adapter_up_weight,
    tenant_of_block,
    slot_of_tenant,
):
    f32, bf16 = jnp.float32, jnp.bfloat16
    blocks = tenant_of_block.shape[0]
    shard_rows, local = attention_input.shape
    own_rows, width = output_gradient.shape
    held, _, rank = adapter_down_weight.shape
    chunks = max(1, own_rows // 32)
    chunk = width // chunks

    slots = jnp.take(slot_of_tenant, tenant_of_block)
    pick = (jnp.arange(dp * held, dtype=jnp.int32)[:, None] == slots[None, :]).astype(f32)
    adapters = jnp.concatenate([jnp.swapaxes(adapter_down_weight, 1, 2), adapter_up_weight], axis=1)
    dma = pltpu.SemaphoreType.DMA
    smem = pl.BlockSpec(memory_space=pltpu.SMEM)
    vmem = pl.BlockSpec(memory_space=pltpu.VMEM)
    anywhere = pl.BlockSpec(memory_space=pl.ANY)
    grad_in, grads = pl.pallas_call(
        functools.partial(kernel, n, dp, chunks),
        out_shape=(
            jax.ShapeDtypeStruct((shard_rows, local), bf16),
            jax.ShapeDtypeStruct((held, 2 * rank, local), f32),
        ),
        in_specs=[smem, smem, vmem, anywhere, anywhere, anywhere],
        out_specs=(anywhere, anywhere),
        scratch_shapes=[
            pltpu.VMEM((chunks, local, chunk), bf16),
            pltpu.VMEM((n, chunks, own_rows, chunk), bf16),
            pltpu.VMEM((n, own_rows, local), f32),
            pltpu.VMEM((shard_rows, local), bf16),
            pltpu.VMEM((dp * held, 2 * rank, local), bf16),
            pltpu.VMEM((blocks, 2 * rank, local), bf16),
            pltpu.VMEM((n, rank, local), bf16),
            pltpu.VMEM((n, rank, own_rows), f32),
            pltpu.VMEM((n, rank, own_rows), f32),
            pltpu.VMEM((n, rank, own_rows), bf16),
            pltpu.VMEM((n, rank, local), bf16),
            pltpu.VMEM((n, rank, local), bf16),
            pltpu.VMEM((blocks, 2 * rank, local), f32),
            pltpu.VMEM((dp, held, 2 * rank, local), bf16),
            pltpu.VMEM((dp, held, 2 * rank, local), bf16),
            pltpu.VMEM((held, 2 * rank, local), f32),
            pltpu.VMEM((n, own_rows, local), bf16),
            dma((chunks,)),
            dma,
            dma((chunks,)),
            dma((2, n - 1, chunks)),
            dma((2, n - 1, chunks)),
            dma((dp - 1,)),
            dma((dp - 1,)),
            dma((4, n - 1)),
            dma((4, n - 1)),
            dma((dp - 1,)),
            dma((dp - 1,)),
            dma((n,)),
            dma,
        ],
        compiler_params=pltpu.CompilerParams(
            collective_id=0, has_side_effects=True, vmem_limit_bytes=62 * 1024 * 1024
        ),
        cost_estimate=pl.CostEstimate(
            flops=2 * shard_rows * width * local,
            bytes_accessed=2 * local * width,
            transcendentals=0,
        ),
        name="gather_and_multiply",
    )(slots, pick, adapters, output_gradient, attention_input, output_weight)
    return grad_in, jnp.swapaxes(grads[:, :rank], 1, 2), grads[:, rank:]


def solution(mesh):
    in_specs = (
        P(("groups", "dp", "tensor"), None),
        P(("groups", "dp"), "tensor"),
        P("tensor", None),
        P("dp", "tensor", None),
        P("dp", None, "tensor"),
        P(("groups", "dp")),
        P(),
    )
    out_specs = (
        P(("groups", "dp"), "tensor"),
        P(("groups", "dp"), "tensor", None),
        P(("groups", "dp"), None, "tensor"),
    )
    sizes = mesh.shape["tensor"], mesh.shape["dp"]

    def per_device(*args):
        return body(*sizes, *args)

    return jax.shard_map(per_device, mesh=mesh, in_specs=in_specs, out_specs=out_specs, check_vma=False)
```

time: 310 us -> 166 us (0.54)
  waiting for transfers between devices: 208 us -> 0 us
  Pallas kernels: 0 us -> 157 us
  local copies, waits for them, and re-layouts: 43.6 us -> 4.4 us
  matrix products: 35.2 us -> 0 us
  between operations: 15 us -> 0.66 us
  blocking collectives: 5.81 us -> 0 us
    all_gather x5 -> x0, waiting for transfers between devices: 175 us -> none  [the longest x1 141 us: body(): rows_piece = lax.all_gather(output_gradient, 'tensor', axis=0, tiled=True)]
    pallas_call x0 -> x1, Pallas kernels: none -> 157 us  [body(): pl.pallas_call(functools.partial(kernel, n, dp, chunks), out_shape=(jax.S...]
    dot_general x8 -> x0, matrix products: 35.2 us -> none  [the longest x1 25.1 us: body(): jnp.einsum('kd,hd->kh', rows_piece, output_weight, preferred_element_type...]
    psum x1 -> x0, waiting for transfers between devices: 32.4 us -> none  [body(): up_flattened = lax.psum(up_part.reshape(block_count, -1), 'tensor')]
    unnamed x29 -> x7, local copies, waits for them, and re-layouts: 28.1 us -> 1.34 us
    reshape x4 -> x0, local copies, waits for them, and re-layouts: 7.82 us -> none  [the longest x1 3.41 us: body(): down_gradient.reshape(held_slot_count, local_width, width_of_rank)]
    unnamed x1 -> x0, blocking collectives: 5.81 us -> none
  transfers between devices with their start and end apart: 6 -> 0, of which waited for: 4 -> 0; matrix products, arithmetic and copies ran while one was open for 18% -> 0% of each run, Pallas kernels for 0% -> 0%
where the time goes in v1:
time: 166 us
  Pallas kernels  157 us (95%)
  local copies, waits for them, and re-layouts  4.4 us (3%)
  other arithmetic  3.8 us (2%)
    pallas_call x1, Pallas kernels, body(): pl.pallas_call(functools.partial(kernel, n, dp, chunks), out_shape=(jax.S...  157 us

profile of v1, /device:TPU:0, one launch (start us, length us, event | category | flops | bytes accessed | tf_op | source)
XLA Modules:
  0.0 166.2 jit_solution(14202728759379362872)
XLA Ops:
  0.6 0.0 copy-start
  0.6 0.7 compare_select_fusion
  1.3 0.0 copy-done
  1.3 0.6 gather_fusion
  2.0 0.7 and_select_fusion.slots_ref
  2.6 0.0 copy-start.2
  2.6 0.6 fusion.pick_ref
  3.2 1.9 %pad_maximum_fusion.adapters_ref = bf16[4,32,2048]{2,1,0:T(8,128)(2,1)} fusion(bf16[4,16,2048]{2,1,0:T(8,128)(2,1)} %param.11, bf16[4,16,2048]{2,1,0:T(8,128)(2,1)} %bitcast.3), kind=kLoop, calls=%fused_computation.1 | loop fusion | flops 1048576 | bytes 1048576 | tf_op jit(solution)/shard_map/concatenate | solution.py:378
  5.1 0.0 copy-done.2
  5.1 157.3 %gather_and_multiply.1 = (bf16[512,2048]{1,0:T(8,128)(2,1)}, f32[4,32,2048]{2,1,0:T(8,128)}) custom-call(s32[4]{0:T(128)} %copy-done.2, f32[16,4]{1,0:T(8,128)} %fusion.pick_ref, bf16[4,32,2048]{2,1,0:T(8,128)(2,1)} %pad_maximum_fusion.adapters_ref, bf16[128,8192]{1,0:T(8,128)(2,1)} %dy_ref.1, bf16[512,2048]{1,0:T(8,128)(2,1)} %x_ref.1, bf16[2048,8192]{1,0:T(8,128)(2,1)} %w_ref.1), custom_call_target="tpu_custom_call" | custom-call | flops 17179869184 | bytes 33554432 | tf_op jit(solution)/shard_map/gather_and_multiply/pallas_call | solution.py:383
  162.4 0.0 copy-start.1
  162.4 2.4 %fusion.1 = (f32[4,16,2048]{2,1,0:T(8,128)}, f32[4,2048,16]{1,2,0:T(8,128)}) fusion(f32[4,32,2048]{2,1,0:T(8,128)} %get-tuple-element.6), kind=kLoop, calls=%fused_computation.8 | loop fusion | bytes 2097152 | tf_op jit(solution)/shard_map/slice | solution.py:433
  164.8 0.0 copy-done.1
  164.8 1.3 copy.11
  (1 shorter events, 0.0 us)
Async XLA Ops:
  0.6 0.7 copy-start
  2.6 2.5 %copy-start.2 = (s32[4]{0:T(128)}, s32[4]{0:T(128)S(1)}, u32[]{:S(2)}) copy-start(s32[4]{0:T(128)S(1)} %and_select_fusion.slots_ref) | copy-start | bytes 52
  162.4 2.4 %copy-start.1 = (bf16[512,2048]{1,0:T(8,128)(2,1)S(1)}, bf16[512,2048]{1,0:T(8,128)(2,1)}, u32[]{:S(2)}) copy-start(bf16[512,2048]{1,0:T(8,128)(2,1)} %get-tuple-element.12) | copy-start | bytes 6291460

commit v2 on v1

--- a/solution.py
+++ b/solution.py
@@ -22,8 +22,8 @@
     n,
     dp,
     chunks,
-    slots_ref,
-    pick_ref,
+    tenant_ref,
+    slot_ref,
     adapters_ref,
     dy_ref,
     x_ref,
@@ -67,8 +67,9 @@
     shard_rows, local = x_ref.shape
     chunk = dy_ref.shape[1] // chunks
     held, rank = adapters_ref.shape[0], adapters_ref.shape[1] // 2
-    blocks = slots_ref.shape[0]
+    blocks = tenant_ref.shape[0]
     per_block = n // blocks
+    slots = [slot_ref[tenant_ref[b]] for b in range(blocks)]
 
     dy_in = [
         pltpu.make_async_copy(dy_ref.at[:, pl.ds(c * chunk, chunk)], rows_v.at[me, c], dy_sem.at[c])
@@ -206,7 +207,7 @@
         for k in range(1, dp):
             adapters_arrival(k).wait_recv()
         for b in range(blocks):
-            selected[b] = all_adapters[slots_ref[b]]
+            selected[b] = all_adapters[slots[b]]
         z_start(0)
         x_in.wait()
         for t in range(n):
@@ -248,9 +249,9 @@
             by_block[b, rank : 2 * rank] = up_sum
 
         def share(slot):
-            value = pick_ref[slot, 0] * by_block[0]
-            for b in range(1, blocks):
-                value = value + pick_ref[slot, b] * by_block[b]
+            value = jnp.zeros((2 * rank, local), f32)
+            for b in range(blocks):
+                value = value + (slots[b] == slot).astype(f32) * by_block[b]
             return value
 
         for k in range(1, dp):
@@ -373,8 +374,6 @@
     chunks = max(1, own_rows // 32)
     chunk = width // chunks
 
-    slots = jnp.take(slot_of_tenant, tenant_of_block)
-    pick = (jnp.arange(dp * held, dtype=jnp.int32)[:, None] == slots[None, :]).astype(f32)
     adapters = jnp.concatenate([jnp.swapaxes(adapter_down_weight, 1, 2), adapter_up_weight], axis=1)
     dma = pltpu.SemaphoreType.DMA
     smem = pl.BlockSpec(memory_space=pltpu.SMEM)
@@ -429,7 +428,7 @@
             transcendentals=0,
         ),
         name="gather_and_multiply",
-    )(slots, pick, adapters, output_gradient, attention_input, output_weight)
+    )(tenant_of_block, slot_of_tenant, adapters, output_gradient, attention_input, output_weight)
     return grad_in, jnp.swapaxes(grads[:, :rank], 1, 2), grads[:, rank:]
 
 

time: 166 us -> 163 us (0.982)
  other arithmetic: 3.8 us -> 1.87 us
where the time goes in v2:
time: 163 us; the launch traced here: 162 us
  Pallas kernels  156 us (96%)
  local copies, waits for them, and re-layouts  3.74 us (2%)
  other arithmetic  1.87 us (1%)
    pallas_call x1, Pallas kernels, body(): pl.pallas_call(functools.partial(kernel, n, dp, chunks), out_shape=(jax.S...  156 us

profile of v2, /device:TPU:0, one launch (start us, length us, event | category | flops | bytes accessed | tf_op | source)
XLA Modules:
  0.0 162.5 jit_solution(4486642853593593698)
XLA Ops:
  0.6 1.9 %pad_maximum_fusion.adapters_ref = bf16[4,32,2048]{2,1,0:T(8,128)(2,1)} fusion(bf16[4,16,2048]{2,1,0:T(8,128)(2,1)} %param.11, bf16[4,16,2048]{2,1,0:T(8,128)(2,1)} %bitcast.3), kind=kLoop, calls=%fused_computation | loop fusion | flops 1048576 | bytes 1048576 | tf_op jit(solution)/shard_map/concatenate | solution.py:377
  2.5 156.2 %gather_and_multiply.1 = (bf16[512,2048]{1,0:T(8,128)(2,1)}, f32[4,32,2048]{2,1,0:T(8,128)}) custom-call(s32[4]{0:T(128)} %tenant_ref.1, s32[16]{0:T(128)} %slot_ref.1, bf16[4,32,2048]{2,1,0:T(8,128)(2,1)} %pad_maximum_fusion.adapters_ref, bf16[128,8192]{1,0:T(8,128)(2,1)} %dy_ref.1, bf16[512,2048]{1,0:T(8,128)(2,1)} %x_ref.1, bf16[2048,8192]{1,0:T(8,128)(2,1)} %w_ref.1), custom_call_target="tpu_custom_call" | custom-call | flops 17179869184 | bytes 33554432 | tf_op jit(solution)/shard_map/gather_and_multiply/pallas_call | solution.py:382
  158.7 0.0 copy-start
  158.7 2.4 %fusion = (f32[4,16,2048]{2,1,0:T(8,128)}, f32[4,2048,16]{1,2,0:T(8,128)}) fusion(f32[4,32,2048]{2,1,0:T(8,128)} %get-tuple-element.6), kind=kLoop, calls=%fused_computation.2 | loop fusion | bytes 2097152 | tf_op jit(solution)/shard_map/slice | solution.py:432
  161.2 0.0 copy-done
  161.2 1.3 copy.11
Async XLA Ops:
  158.7 2.4 %copy-start = (bf16[512,2048]{1,0:T(8,128)(2,1)S(1)}, bf16[512,2048]{1,0:T(8,128)(2,1)}, u32[]{:S(2)}) copy-start(bf16[512,2048]{1,0:T(8,128)(2,1)} %get-tuple-element.12) | copy-start | bytes 6291460
